TPU v7x, 256 devices: a whole 4x4x8 slice. The times are simulated.
256 devices in a mesh: occ: 128 (over x_lo, z, y, core), aux: 2 (over x_hi).
Axes of the slice: x: 4 (x_hi: 2, x_lo: 2; x = x_hi * 2 + x_lo), y: 4, z: 8, core: 2. Of those that a mesh axis runs over, the one named last changes fastest.
Arguments:
- cholesky: bfloat16 [128, 5120, 1024], P('occ', 'aux'), may hold values from -0.099609375 to 0.099609375
- occ_energy: float32 [128], replicated, may hold values from -1.5 to -0.4
- vir_energy: float32 [1024], replicated, may hold values from 0.3 to 4
Outputs:
- vir_density: float32 [1024, 1024], P('occ', 'aux')
- occ_diagonal: float32 [128], P('occ')
All inputs are finite; a program needn't handle non-finite values.
Results may differ from a plain program's by a relative error of at most 0.0044.
Values may be sent and summed in bfloat16 or wider, within the bound.
A program may use at most 64 MiB of HBM per device.

v0:
```python
import jax
import jax.numpy as jnp
from jax import lax
from jax.sharding import PartitionSpec as P

STEPS = 2


def from_behind(block, axis, distance):
    devices = range(lax.axis_size(axis))
    route = [((i - distance) % len(devices), i) for i in devices]
    return lax.ppermute(block, axis, route)


def density_term(amplitudes, tildes, chosen):
    total = None
    for which in chosen:
        rows = amplitudes[which]
        piece = 2.0 * lax.dot_general(
            rows, tildes[which], (((1,), (1,)), ((), ())), preferred_element_type=jnp.float32
        )
        total = piece if total is None else total + piece
    return total


def per_device(cholesky, occ_energy, vir_energy):
    own_block = cholesky[0]
    number = lax.axis_size("occ")
    center = lax.axis_index("occ")
    halves = lax.axis_size("aux")
    half_index = lax.axis_index("aux")
    vir_count = own_block.shape[1]
    half_rows = vir_count // halves
    row_start = half_index * half_rows
    center_energy = lax.dynamic_index_in_dim(occ_energy, center, 0, keepdims=False)
    vir_half = lax.dynamic_slice_in_dim(vir_energy, row_start, half_rows)
    pair_half = vir_half[:, None] + vir_energy[None, :]
    partners = []
    moving = own_block
    for offset in range(STEPS):
        moving = from_behind(moving, "occ", -1)
        partners.append(moving)
    amplitudes = []
    tildes = []
    totals = []
    for offset in range(1, STEPS + 1):
        right_block = partners[offset - 1]
        partner_energy = lax.dynamic_index_in_dim(
            occ_energy, (center + offset) % number, 0, keepdims=False
        )

        def integral_rows(first_row, row_count, right_block=right_block):
            return lax.dot_general(
                own_block, right_block, (((0,), (0,)), ((), ())), preferred_element_type=jnp.float32
            )

        integrals = lax.psum_scatter(
            integral_rows(jnp.int32(0), half_rows * lax.axis_size("aux")).astype(jnp.bfloat16),
            "aux",
            scatter_dimension=0,
            tiled=True,
        ).astype(jnp.float32)
        amp_half = (integrals / (pair_half - center_energy - partner_energy)).astype(jnp.bfloat16)
        amplitude = lax.all_gather(amp_half, "aux", axis=0, tiled=True)
        wide = amplitude.astype(jnp.float32)
        tilde = (2.0 * wide - wide.T).astype(jnp.bfloat16)
        amplitudes.append(amplitude)
        tildes.append(lax.dynamic_slice_in_dim(tilde, row_start, half_rows, 0))
        totals.append(-(2.0 / vir_count) * jnp.sum(wide * tilde.astype(jnp.float32)))
    vir_density = lax.psum_scatter(
        density_term(amplitudes, tildes, list(range(STEPS))), "occ", scatter_dimension=0, tiled=True
    )
    band = jnp.stack(totals)
    diagonal = jnp.zeros((1,), jnp.float32)
    for offset in range(1, STEPS + 1):
        arrived = from_behind(band, "occ", offset)
        diagonal = diagonal + arrived[offset - 1]
    return (vir_density, diagonal)


def solution(mesh):
    in_specs = (P("occ", "aux", None), P(), P())
    out_specs = (P("occ", "aux"), P("occ"))
    return jax.shard_map(
        per_device, mesh=mesh, in_specs=in_specs, out_specs=out_specs, check_vma=False
    )
```

profile of v0, /device:TPU:2, one launch (start us, length us, event | category | flops | bytes accessed | tf_op | source)
XLA Modules:
  0.0 873.1 jit_solution(11583814203628534614)
XLA Ops:
  7.2 7.8 collective-permute-start
  15.0 57.6 %collective-permute-done = bf16[2560,1024]{1,0:T(8,128)(2,1)} collective-permute-done((bf16[2560,1024]{1,0:T(8,128)(2,1)}, bf16[2560,1024]{1,0:T(8,128)(2,1)}, u32[]{:S(2)}, u32[]{:S(2)}) %collective-permute-start) | collective-permute-done | bytes 5242912 | tf_op jit(solution)/shard_map/ppermute | solution.py:12
  72.6 6.1 collective-permute-start.1
  78.7 10.2 %convolution_convert_fusion.1 = bf16[1024,1024]{1,0:T(8,128)(2,1)} fusion(bf16[2560,1024]{1,0:T(8,128)(2,1)} %collective-permute-done, bf16[1,2560,1024]{2,1,0:T(8,128)(2,1)} %param.3), kind=kOutput, calls=%fused_computation.14 | convolution fusion | flops 5369757696 | bytes 12582912 | tf_op jit(solution)/shard_map/dot_general | solution.py:53
  88.9 0.0 reduce-scatter.6.cloned.1.call-start
  88.9 47.4 %collective-permute-done.1 = bf16[2560,1024]{1,0:T(8,128)(2,1)} collective-permute-done((bf16[2560,1024]{1,0:T(8,128)(2,1)}, bf16[2560,1024]{1,0:T(8,128)(2,1)}, u32[]{:S(2)}, u32[]{:S(2)}) %collective-permute-start.1) | collective-permute-done | bytes 5242912 | tf_op jit(solution)/shard_map/ppermute | solution.py:12
  136.3 10.1 %convolution_convert_fusion = bf16[1024,1024]{1,0:T(8,128)(2,1)} fusion(bf16[2560,1024]{1,0:T(8,128)(2,1)} %collective-permute-done.1, bf16[1,2560,1024]{2,1,0:T(8,128)(2,1)} %param.3), kind=kOutput, calls=%fused_computation.13 | convolution fusion | flops 5369757696 | bytes 12582912 | tf_op jit(solution)/shard_map/dot_general | solution.py:53
  146.5 0.0 all-gather.5.cloned.1.call-start
  146.5 0.6 copy-done.3
  147.1 0.1 dynamic_slice.19
  147.2 0.7 fusion.13
  147.8 50.1 %reduce-scatter.6.cloned.1.call-done = bf16[512,1024]{1,0:T(8,128)(2,1)} async-done(((bf16[1024,1024]{1,0:T(8,128)(2,1)}), bf16[512,1024]{1,0:T(8,128)(2,1)}) %reduce-scatter.6.cloned.1.call-update) | async-done | bytes 1048592 | tf_op jit(solution)/shard_map/reduce_scatter | solution.py:57
  198.0 5.7 divide_convert_fusion
  203.7 0.5 all-gather.3.cloned.1.call-update
  204.2 0.2 reduce-scatter.8.cloned.1.call-start
  204.5 38.5 %all-gather.5.cloned.1.call-done = bf16[1024,1024]{1,0:T(8,128)(2,1)} async-done(((bf16[512,1024]{1,0:T(8,128)(2,1)}), bf16[1024,1024]{1,0:T(8,128)(2,1)}) %all-gather.5.cloned.1.call-update) | async-done | bytes 2097168 | tf_op jit(solution)/shard_map/all_gather | solution.py:64
  243.0 4.1 convert_bitcast_fusion
  247.1 5.4 copy.6
  252.6 31.3 %all-gather.3.cloned.1.call-done = bf16[1024,1024]{1,0:T(8,128)(2,1)} async-done(((bf16[512,1024]{1,0:T(8,128)(2,1)}), bf16[1024,1024]{1,0:T(8,128)(2,1)}) %all-gather.3.cloned.1.call-update) | async-done | bytes 2097168 | tf_op jit(solution)/shard_map/all_gather | solution.py:64
  283.9 4.3 copy.5
  288.2 4.0 multiply_reduce_fusion
  292.2 1.3 fusion.5
  293.5 0.9 copy-done
  294.4 0.7 copy-done.1
  295.1 2.2 fusion.2
  297.3 2.6 add_multiply_fusion
  301.2 0.1 pad_maximum_fusion
  301.3 1.5 collective-permute-start.3
  302.8 6.4 collective-permute-done.3
  309.2 0.6 slice.7
  309.8 0.2 collective-permute-done.2
  310.7 554.8 %reduce-scatter.8.cloned.1.call-done = f32[8,512]{1,0:T(8,128)} async-done(((f32[1024,512]{1,0:T(8,128)}), f32[8,512]{1,0:T(8,128)}) %reduce-scatter.8.cloned.1.call-update) | async-done | bytes 16400 | tf_op jit(solution)/shard_map/reduce_scatter | solution.py:70
  (15 shorter events, 0.2 us)
Async XLA Ops:
  7.2 140.7 %reduce-scatter.4.cloned.1.call-start = ((), (), s32[]{:S(2)}) async-start(), calls=%async_computation.3 | async-start | bytes 3145728 | tf_op jit(solution)/shard_map/reduce_scatter | solution.py:57
  7.2 65.4 %collective-permute-start = (bf16[2560,1024]{1,0:T(8,128)(2,1)}, bf16[2560,1024]{1,0:T(8,128)(2,1)}, u32[]{:S(2)}, u32[]{:S(2)}) collective-permute-start(bf16[2560,1024]{1,0:T(8,128)(2,1)} %bitcast.22), channel_id=1, source_target_pairs={{2,0},{4,2},{6,4},{8,6},{10,8},{12,10},{14,12},{16,14},{18,16},{20... | collective-permute-start | bytes 15728648 | tf_op jit(solution)/shard_map/ppermute | solution.py:12
  72.6 63.7 %collective-permute-start.1 = (bf16[2560,1024]{1,0:T(8,128)(2,1)}, bf16[2560,1024]{1,0:T(8,128)(2,1)}, u32[]{:S(2)}, u32[]{:S(2)}) collective-permute-start(bf16[2560,1024]{1,0:T(8,128)(2,1)} %collective-permute-done), channel_id=1, source_target_pairs={{2,0},{4,2},{6,4},{8,6},{10,8},{12,10},{14,12},{16,14},{18,16},{20... | collective-permute-start | bytes 15728648 | tf_op jit(solution)/shard_map/ppermute | solution.py:12
  88.9 109.1 %reduce-scatter.6.cloned.1.call-start = ((), (), s32[]{:S(2)}) async-start(), calls=%async_computation.5 | async-start | bytes 3145728 | tf_op jit(solution)/shard_map/reduce_scatter | solution.py:57
  146.4 0.7 copy-start.3
  146.4 0.8 copy-start.4
  146.5 96.5 %all-gather.5.cloned.1.call-start = ((), (), s32[]{:S(2)}) async-start(), calls=%async_computation.6 | async-start | bytes 3145728 | tf_op jit(solution)/shard_map/all_gather | solution.py:64
  203.7 80.2 %all-gather.3.cloned.1.call-start = ((), (), s32[]{:S(2)}) async-start(), calls=%async_computation.4 | async-start | bytes 3145728 | tf_op jit(solution)/shard_map/all_gather | solution.py:64
  204.2 661.2 %reduce-scatter.8.cloned.1.call-start = ((), (), s32[]{:S(2)}) async-start(), calls=%async_computation.7 | async-start | bytes 2113536 | tf_op jit(solution)/shard_map/reduce_scatter | solution.py:70
  283.8 4.3 copy-start.2
  292.2 2.2 copy-start
  292.2 2.9 copy-start.1
  301.3 7.9 collective-permute-start.3
  302.8 7.2 collective-permute-start.2
Sparse Core Ops, SparseCore 0:
  89.0 31.8 reduce-scatter.3
  146.6 51.3 reduce-scatter.5
  203.8 39.1 all-gather.4
  244.6 39.1 all-gather.2
  300.1 565.3 reduce-scatter.7
where the time goes:
time: 874 us; the launch traced here: 873 us
  waiting for transfers between devices  787 us (90%)
  matrix products  24.2 us (3%)
  between operations  16.9 us (2%)
  other arithmetic  16.1 us (2%)
  starting transfers between devices  15.8 us (2%)
  local copies, waits for them, and re-layouts  13.2 us (2%)
    reduce_scatter x1, waiting for transfers between devices, per_device(): lax.psum_scatter(density_term(amplitudes, tildes, list(range(STEPS))), 'o...  555 us
    ppermute x4, waiting for transfers between devices, from_behind(): return lax.ppermute(block, axis, route)  112 us
    all_gather x2, waiting for transfers between devices, per_device(): amplitude = lax.all_gather(amp_half, 'aux', axis=0, tiled=True)  69.8 us
    reduce_scatter x2, waiting for transfers between devices, per_device(): lax.psum_scatter(integral_rows(jnp.int32(0), half_rows * lax.axis_size('a...  50.1 us
    dot_general x2, matrix products, integral_rows(): lax.dot_general(own_block, right_block, (((0,), (0,)), ((), ())), preferr...  20.3 us
  transfers between devices with their start and end apart: 9, of which 8 were waited for; matrix products, arithmetic and copies ran while one was open for 4% of the time, Pallas kernels for 0%

commit v1 on v0

v1 whole, which is shorter than its diff:
```python
import functools

import jax
import jax.numpy as jnp
from jax import lax
from jax.experimental import pallas as pl
from jax.experimental.pallas import tpu as pltpu
from jax.sharding import PartitionSpec as P

MESH = pl.DeviceIdType.MESH
NAUX_HALF = 2560
NVIR = 1024
NOCC = 128
NC = 8
CW = NVIR // NC
HALF = NVIR // 2
f32 = jnp.float32
bf16 = jnp.bfloat16


def kernel(
    x_ref, eocc_ref, v_ref, dens_ref, diag_ref,
    own, own_t, blocks, sendb, recvb, acc, lr, tt, dens, dens_in, sx, rx, fsum, ry, gsum, rz, tbuf, colv,
    own_sem, ys, yr, ds, dr, xs, xr, cs, cr, qs, qr, us, ur, zs, zr, ts, tr,
):
    k = lax.axis_index("occ")
    h = lax.axis_index("aux")
    core = lax.rem(k, 2)
    y = lax.rem(k // 2, 4)
    z = lax.rem(k // 8, 8)
    x = h * 2 + k // 64
    inner = lax.rem(k, 64)

    def x_place(d):
        to = lax.rem(x + d, 4)
        return {"occ": lax.rem(to, 2) * 64 + inner, "aux": to // 2}

    def y_place(d):
        return {"occ": k + (lax.rem(y + d, 4) - y) * 2, "aux": h}

    def z_place(d):
        return {"occ": k + (lax.rem(z + d, 8) - z) * 8, "aux": h}

    above = {"occ": lax.rem(k + 2, NOCC), "aux": h}
    below = {"occ": lax.rem(k + NOCC - 2, NOCC), "aux": h}
    sibling = {"occ": k + 1 - 2 * core, "aux": h}
    partner = {"occ": k, "aux": 1 - h}
    onward = {"occ": lax.rem(k + NOCC - 2 + 4 * core, NOCC), "aux": h}

    def remote(src, dst, send, recv, device):
        return pltpu.make_async_remote_copy(
            src_ref=src, dst_ref=dst, send_sem=send, recv_sem=recv, device_id=device, device_id_type=MESH
        )

    load = pltpu.make_async_copy(x_ref.at[0], own, own_sem)
    load.start()

    barrier = pltpu.get_barrier_semaphore()
    greeted = [above, below, sibling, partner, x_place(1), x_place(3)]
    greeted += [y_place(d) for d in range(1, 4)] + [z_place(d) for d in range(1, 8)]
    for device in greeted:
        pl.semaphore_signal(barrier, inc=1, device_id=device, device_id_type=MESH)
    pl.semaphore_wait(barrier, len(greeted))

    def columns(j):
        return pl.ds(pl.multiple_of(j * CW, CW), CW)

    def ring_copy(j):
        return remote(x_ref.at[0, :, columns(j)], blocks.at[0, j], ys.at[j], yr.at[j], onward)

    def own_copy(j):
        return remote(x_ref.at[0, :, columns(j)], blocks.at[1, j], ds.at[j], dr.at[j], sibling)

    def pass_copy(j):
        return remote(blocks.at[0, j], blocks.at[1, j], ds.at[j], dr.at[j], sibling)

    def pair_copy(j):
        return remote(sendb.at[j], recvb.at[j], xs.at[j], xr.at[j], partner)

    @pl.loop(0, NC)
    def _(j):
        ring_copy(j).start()

        @pl.when(core == 0)
        def _():
            own_copy(j).start()

    for m in range(8):
        row = v_ref[0:1, m * 128:(m + 1) * 128]
        colv[m * 128:(m + 1) * 128, :] = jnp.broadcast_to(row, (128, 128)).T

    load.wait()

    @pl.loop(0, NAUX_HALF // 128)
    def _(i):
        rows = pl.ds(pl.multiple_of(i * 128, 128), 128)
        own_t[:, rows] = own[rows, :].T

    center = lax.rem(k - h - 2 * core * (1 - h) + NOCC, NOCC)
    other = lax.rem(center + 2 - h, NOCC)
    center_energy = eocc_ref[center]
    other_energy = eocc_ref[other]
    place = 1 - (1 - core) * (1 - h)

    def finish(j):
        pair_copy(j).wait_recv()
        vrow = v_ref[0:1, columns(j)]

        @pl.loop(0, 8)
        def _(m):
            rows = pl.ds(pl.multiple_of(m * 128, 128), 128)
            total = acc[j, rows, :] + recvb[j, rows, :].astype(f32)
            part = total / (colv[rows, :] + vrow - center_energy - other_energy)
            lr[place, rows, columns(j)] = part.astype(bf16)
            lr[1 - place, columns(j), rows] = part.T.astype(bf16)

    @pl.loop(0, NC + 1)
    def _(j):
        @pl.when(j < NC)
        def _():
            ring_copy(j).wait_recv()

            @pl.when(core == 1)
            def _():
                pass_copy(j).start()

            own_copy(j).wait_recv()
            for m in range(4):
                rows = pl.ds(m * 256, 256)
                sendb[j, rows, :] = jnp.dot(
                    own_t[rows, :], blocks[1 - h, j], preferred_element_type=f32
                ).astype(bf16)
            pair_copy(j).start()
            for m in range(4):
                rows = pl.ds(m * 256, 256)
                acc[j, rows, :] = jnp.dot(own_t[rows, :], blocks[h, j], preferred_element_type=f32)

        @pl.when(j > 0)
        def _():
            finish(j - 1)

    def tilde_rows(i, term):
        rows = pl.ds(pl.multiple_of(i * 128, 128), 128)
        left = lr[0, rows, :].astype(f32)
        right = lr[1, rows, :].astype(f32)
        tilde = (2.0 * right - left).astype(bf16)
        tt[rows, :] = tilde
        return term + jnp.sum((right * tilde.astype(f32)).reshape(16, 8, 8, 128), axis=(0, 2))

    term = lax.fori_loop(0, 8, tilde_rows, jnp.zeros((8, 128), f32))
    tbuf[h] = jnp.full((8, 128), -(2.0 / NVIR) * jnp.sum(term), f32)
    term_copy = remote(tbuf.at[h], tbuf.at[h], ts.at[0], tr.at[0], partner)
    term_copy.start()

    @pl.loop(0, 4)
    def _(i):
        rows = pl.ds(pl.multiple_of(i * 256, 256), 256)
        out = 2.0 * jnp.dot(lr[0, rows, :], tt[...], preferred_element_type=f32)
        dens[pl.ds(i * 16, 16)] = out.reshape(16, 2, 8, NVIR)

    core_copy = remote(dens.at[:, 1 - core], dens_in, cs, cr, sibling)
    core_copy.start()
    core_copy.wait_recv()

    x_copies = []
    for d in (2, 1, 3, 0):
        to = lax.rem(x + d, 4)
        groups = pl.ds(lax.rem(to, 2) * 32, 32)
        cols = pl.ds(pl.multiple_of((to // 2) * HALF, HALF), HALF)
        both = dens[groups, core, :, cols] + dens_in[groups, :, cols]
        if d == 0:
            fsum[...] = both
        else:
            sx[d - 1] = both.reshape(256, HALF).astype(bf16)
            copy = remote(sx.at[d - 1], rx.at[d - 1], qs.at[d - 1], qr.at[d - 1], x_place(d))
            copy.start()
            x_copies.append(copy)

    term_copy.wait()
    step_copy = remote(tbuf.at[0], tbuf.at[2], ts.at[1], tr.at[1], above)
    step_copy.start()

    for copy in x_copies:
        copy.wait_recv()
    fsum[...] += (rx[0].astype(f32) + rx[1].astype(f32) + rx[2].astype(f32)).reshape(32, 8, HALF)

    def y_part(to):
        return fsum.reshape(8, 4, 8, HALF).at[:, to]

    y_copies = []
    for d in (2, 1, 3):
        copy = remote(y_part(lax.rem(y + d, 4)), ry.at[d - 1], us.at[d - 1], ur.at[d - 1], y_place(d))
        copy.start()
        y_copies.append(copy)
    for copy in y_copies:
        copy.wait_recv()
    gsum[...] = y_part(y)[...] + ry[0] + ry[1] + ry[2]

    z_copies = []
    for d in (4, 3, 5, 2, 6, 1, 7):
        copy = remote(gsum.at[lax.rem(z + d, 8)], rz.at[d - 1], zs.at[d - 1], zr.at[d - 1], z_place(d))
        copy.start()
        z_copies.append(copy)

    step_copy.wait_recv()
    diag_ref[...] = tbuf[1] + jnp.where(core == 0, tbuf[2], tbuf[0])

    for copy in z_copies:
        copy.wait_recv()
    total = gsum[z]
    for d in range(7):
        total = total + rz[d]
    dens_ref[...] = total

    step_copy.wait_send()
    core_copy.wait_send()
    for copy in x_copies + y_copies + z_copies:
        copy.wait_send()

    @pl.loop(0, NC)
    def _(j):
        ring_copy(j).wait_send()
        own_copy(j).wait_send()
        pair_copy(j).wait_send()


def per_device(cholesky, occ_energy, vir_energy):
    dma = pltpu.SemaphoreType.DMA
    vmem = pltpu.VMEM
    dens, diag = pl.pallas_call(
        kernel,
        out_shape=(jax.ShapeDtypeStruct((8, HALF), f32), jax.ShapeDtypeStruct((8, 128), f32)),
        in_specs=[
            pl.BlockSpec(memory_space=pl.ANY),
            pl.BlockSpec(memory_space=pltpu.SMEM),
            pl.BlockSpec(memory_space=pltpu.VMEM),
        ],
        out_specs=(pl.BlockSpec(memory_space=pltpu.VMEM), pl.BlockSpec(memory_space=pltpu.VMEM)),
        scratch_shapes=[
            vmem((NAUX_HALF, NVIR), bf16),
            vmem((NVIR, NAUX_HALF), bf16),
            vmem((2, NC, NAUX_HALF, CW), bf16),
            vmem((NC, NVIR, CW), bf16),
            vmem((NC, NVIR, CW), bf16),
            vmem((NC, NVIR, CW), f32),
            vmem((2, NVIR, NVIR), bf16),
            vmem((NVIR, NVIR), bf16),
            vmem((64, 2, 8, NVIR), f32),
            vmem((64, 8, NVIR), f32),
            vmem((3, 256, HALF), bf16),
            vmem((3, 256, HALF), bf16),
            vmem((32, 8, HALF), f32),
            vmem((3, 8, 8, HALF), f32),
            vmem((8, 8, HALF), f32),
            vmem((7, 8, HALF), f32),
            vmem((3, 8, 128), f32),
            vmem((NVIR, 128), f32),
            dma(()),
            dma((NC,)), dma((NC,)), dma((NC,)), dma((NC,)), dma((NC,)), dma((NC,)),
            dma(()), dma(()),
            dma((3,)), dma((3,)), dma((3,)), dma((3,)), dma((7,)), dma((7,)), dma((2,)), dma((2,)),
        ],
        compiler_params=pltpu.CompilerParams(
            collective_id=0, has_side_effects=True, vmem_limit_bytes=58 * 2**20
        ),
        cost_estimate=pl.CostEstimate(flops=13_000_000_000, bytes_accessed=16_000_000, transcendentals=0),
    )(cholesky, occ_energy, vir_energy.reshape(1, NVIR))
    return dens, diag[0, :1]


def solution(mesh):
    in_specs = (P("occ", "aux", None), P(), P())
    out_specs = (P("occ", "aux"), P("occ"))
    return jax.shard_map(
        per_device, mesh=mesh, in_specs=in_specs, out_specs=out_specs, check_vma=False
    )
```

time: 874 us -> 154 us (0.18)
  the two profiles are of different devices: /device:TPU:2 before, /device:TPU:10 now
where the time goes in v1:
time: 154 us
  Pallas kernels  151 us (98%)
  local copies, waits for them, and re-layouts  2.51 us (2%)
    pallas_call x1, Pallas kernels, per_device(): pl.pallas_call(kernel, out_shape=(jax.ShapeDtypeStruct((8, HALF), f32), j...  151 us

profile of v1, /device:TPU:10, one launch (start us, length us, event | category | flops | bytes accessed | tf_op | source)
XLA Modules:
  0.0 154.0 jit_solution(11725755251356420107)
XLA Ops:
  0.6 150.8 %shard_map.50 = (f32[8,512]{1,0:T(8,128)}, f32[8,128]{1,0:T(8,128)}) custom-call(bf16[1,2560,1024]{2,1,0:T(8,128)(2,1)} %x_ref.1, f32[128]{0:T(128)} %eocc_ref.1, f32[1,1024]{1,0:T(1,128)} %bitcast.2), custom_call_target="tpu_custom_call" | custom-call | flops 12999999488 | bytes 16000000 | tf_op jit(solution)/shard_map/pallas_call | solution.py:230
  151.5 1.2 slice.3
  152.7 1.3 copy.6

commit v2 on v1

--- a/solution.py
+++ b/solution.py
@@ -14,14 +14,16 @@
 NC = 8
 CW = NVIR // NC
 HALF = NVIR // 2
+QUARTER = NVIR // 4
 f32 = jnp.float32
 bf16 = jnp.bfloat16
 
 
 def kernel(
     x_ref, eocc_ref, v_ref, dens_ref, diag_ref,
-    own, own_t, blocks, sendb, recvb, acc, lr, tt, dens, dens_in, sx, rx, fsum, ry, gsum, rz, tbuf, colv,
-    own_sem, ys, yr, ds, dr, xs, xr, cs, cr, qs, qr, us, ur, zs, zr, ts, tr,
+    own, own_t, blocks, relay, sendb, recvb, acc, lr, tt, dens, dens_in,
+    first_out, first_in, second_out, second_in, xsum, ysum, gsum, rz, tbuf, colv,
+    own_sem, ys, yr, ds, dr, xs, xr, ls, lw, cs, cr, fs, fr, us, ur, zs, zr, ts, tr,
 ):
     k = lax.axis_index("occ")
     h = lax.axis_index("aux")
@@ -47,6 +49,23 @@
     partner = {"occ": k, "aux": 1 - h}
     onward = {"occ": lax.rem(k + NOCC - 2 + 4 * core, NOCC), "aux": h}
 
+    up = core == 1
+    low = k // 64
+    row, level = jnp.where(up, y, 3 - y), jnp.where(up, z, 7 - z)
+
+    def corner_place(low, row, level):
+        inner = jnp.where(up, level * 8 + row * 2, (7 - level) * 8 + (3 - row) * 2) + core
+        return {"occ": low * 64 + inner, "aux": h}
+
+    def at(row_is, level_is):
+        return (row == row_is) & (level == level_is)
+
+    leaves, meets = at(3, 7), at(0, 0)
+    early_a, early_b, late_a, late_b = at(3, 4), at(3, 5), at(3, 1), at(3, 2)
+    hands_on = early_a | early_b
+    hands_in = meets | late_a | late_b
+    relay_from = jnp.where(early_a, 1, jnp.where(late_a, 3, jnp.where(late_b, 2, 0)))
+
     def remote(src, dst, send, recv, device):
         return pltpu.make_async_remote_copy(
             src_ref=src, dst_ref=dst, send_sem=send, recv_sem=recv, device_id=device, device_id_type=MESH
@@ -60,7 +79,26 @@
     greeted += [y_place(d) for d in range(1, 4)] + [z_place(d) for d in range(1, 8)]
     for device in greeted:
         pl.semaphore_signal(barrier, inc=1, device_id=device, device_id_type=MESH)
-    pl.semaphore_wait(barrier, len(greeted))
+
+    def greet(device):
+        pl.semaphore_signal(barrier, inc=1, device_id=device, device_id_type=MESH)
+
+    @pl.when(meets)
+    def _():
+        greet(corner_place(low, 3, 7))
+        greet(corner_place(low, 3, 1))
+        greet(corner_place(low, 3, 2))
+
+    @pl.when(hands_on)
+    def _():
+        greet(corner_place(1 - low, 3, 7))
+
+    @pl.when(late_a | late_b)
+    def _():
+        greet(corner_place(low, 3, level + 3))
+
+    more = jnp.where(leaves, 3, jnp.where(hands_on | late_a | late_b, 1, 0))
+    pl.semaphore_wait(barrier, len(greeted) + more)
 
     def columns(j):
         return pl.ds(pl.multiple_of(j * CW, CW), CW)
@@ -68,6 +106,21 @@
     def ring_copy(j):
         return remote(x_ref.at[0, :, columns(j)], blocks.at[0, j], ys.at[j], yr.at[j], onward)
 
+    def relay_copy(j):
+        place = corner_place(
+            jnp.where(j < 4, low, 1 - low), jnp.where(j < 4, 0, 3), jnp.where(j < 4, 0, 5 - lax.rem(j, 2))
+        )
+        slot = lax.rem(j // 2, 2)
+        return remote(x_ref.at[0, :, columns(j)], relay.at[slot], ys.at[j], lw.at[slot], place)
+
+    def handed_on(i):
+        return remote(relay.at[i], relay.at[i], ls.at[i], lw.at[i], corner_place(low, 3, level - 3))
+
+    def handed_in(i):
+        j = 2 * i + jnp.where(meets, 1, jnp.where(late_a, 5, 4))
+        place = corner_place(jnp.where(meets, 1 - low, low), 0, 0)
+        return remote(relay.at[i], blocks.at[0, j], ls.at[i], yr.at[j], place)
+
     def own_copy(j):
         return remote(x_ref.at[0, :, columns(j)], blocks.at[1, j], ds.at[j], dr.at[j], sibling)
 
@@ -79,7 +132,17 @@
 
     @pl.loop(0, NC)
     def _(j):
-        ring_copy(j).start()
+        i = j // 2
+        chunk = jnp.where(leaves, jnp.where(lax.rem(j, 2) == 0, i + 1 - 2 * lax.rem(i, 2), 4 + i), j)
+        by_relay = leaves & ((chunk >= 4) | (lax.rem(chunk, 2) == 1))
+
+        @pl.when(by_relay)
+        def _():
+            relay_copy(chunk).start()
+
+        @pl.when(jnp.logical_not(by_relay))
+        def _():
+            ring_copy(chunk).start()
 
         @pl.when(core == 0)
         def _():
@@ -114,26 +177,60 @@
             lr[place, rows, columns(j)] = part.astype(bf16)
             lr[1 - place, columns(j), rows] = part.T.astype(bf16)
 
-    @pl.loop(0, NC + 1)
-    def _(j):
-        @pl.when(j < NC)
+    def product(stream, j):
+        @pl.when(stream == 0)
         def _():
             ring_copy(j).wait_recv()
 
-            @pl.when(core == 1)
+            @pl.when(up)
             def _():
                 pass_copy(j).start()
 
+            turn = j - relay_from
+            slot = lax.rem(jnp.maximum(turn, 0) // 2, 2)
+
+            @pl.when((hands_on | hands_in) & (turn >= 0) & (turn < 4) & (lax.rem(turn + 8, 2) == 0))
+            def _():
+                handed_on(slot).wait_recv()
+
+                @pl.when(hands_on)
+                def _():
+                    handed_on(slot).start()
+
+                @pl.when(hands_in)
+                def _():
+                    handed_in(slot).start()
+
+        @pl.when(stream == 1)
+        def _():
             own_copy(j).wait_recv()
+
+        @pl.when(stream == h)
+        def _():
+            for m in range(4):
+                rows = pl.ds(m * 256, 256)
+                acc[j, rows, :] = jnp.dot(own_t[rows, :], blocks[stream, j], preferred_element_type=f32)
+
+        @pl.when(stream != h)
+        def _():
             for m in range(4):
                 rows = pl.ds(m * 256, 256)
                 sendb[j, rows, :] = jnp.dot(
-                    own_t[rows, :], blocks[1 - h, j], preferred_element_type=f32
+                    own_t[rows, :], blocks[stream, j], preferred_element_type=f32
                 ).astype(bf16)
             pair_copy(j).start()
-            for m in range(4):
-                rows = pl.ds(m * 256, 256)
-                acc[j, rows, :] = jnp.dot(own_t[rows, :], blocks[h, j], preferred_element_type=f32)
+
+    @pl.loop(0, NC + 1)
+    def _(j):
+        @pl.loop(0, 3)
+        def _(q):
+            early = up & (q < 2)
+            stream = jnp.where(up, jnp.where(early, 1, 0), jnp.where(q == 0, 1 - h, h))
+            chunk = jnp.where(early, 2 * j + q, j)
+
+            @pl.when((j < NC) & jnp.where(up, (q == 2) | (j < NC // 2), q < 2))
+            def _():
+                product(stream, chunk)
 
         @pl.when(j > 0)
         def _():
@@ -152,49 +249,77 @@
     term_copy = remote(tbuf.at[h], tbuf.at[h], ts.at[0], tr.at[0], partner)
     term_copy.start()
 
+    def core_copy(i):
+        rows = pl.ds(i * 4, 4)
+        return remote(dens.at[rows, :, 1 - core], dens_in.at[rows], cs.at[i], cr.at[i], sibling)
+
     @pl.loop(0, 4)
     def _(i):
         rows = pl.ds(pl.multiple_of(i * 256, 256), 256)
         out = 2.0 * jnp.dot(lr[0, rows, :], tt[...], preferred_element_type=f32)
-        dens[pl.ds(i * 16, 16)] = out.reshape(16, 2, 8, NVIR)
-
-    core_copy = remote(dens.at[:, 1 - core], dens_in, cs, cr, sibling)
-    core_copy.start()
-    core_copy.wait_recv()
-
-    x_copies = []
-    for d in (2, 1, 3, 0):
-        to = lax.rem(x + d, 4)
-        groups = pl.ds(lax.rem(to, 2) * 32, 32)
-        cols = pl.ds(pl.multiple_of((to // 2) * HALF, HALF), HALF)
-        both = dens[groups, core, :, cols] + dens_in[groups, :, cols]
-        if d == 0:
-            fsum[...] = both
-        else:
-            sx[d - 1] = both.reshape(256, HALF).astype(bf16)
-            copy = remote(sx.at[d - 1], rx.at[d - 1], qs.at[d - 1], qr.at[d - 1], x_place(d))
-            copy.start()
-            x_copies.append(copy)
+        dens[pl.ds(i * 4, 4)] = out.reshape(4, 4, 2, 8, NVIR)
+        core_copy(i).start()
+
+    @pl.loop(0, 4)
+    def _(i):
+        core_copy(i).wait_recv()
+
+    def x_term(to):
+        rows = pl.ds(lax.rem(to, 2) * 8, 8)
+        cols = pl.ds(pl.multiple_of((to // 2) * HALF, QUARTER), QUARTER)
+        return dens[rows, :, core, :, cols] + dens_in[rows, :, :, cols]
+
+    def y_term(to, side):
+        cols = pl.ds(side * HALF + QUARTER, QUARTER)
+        return dens[:, to, core, :, cols] + dens_in[:, to, :, cols]
+
+    def first_copy(way, d):
+        i = way * 3 + d - 1
+        to = y_place(d) if way else x_place(d)
+        return remote(first_out.at[way, d - 1], first_in.at[way, d - 1], fs.at[i], fr.at[i], to)
+
+    for d in (2, 1, 3):
+        first_out[0, d - 1] = x_term(lax.rem(x + d, 4)).reshape(256, QUARTER).astype(bf16)
+        first_copy(0, d).start()
+        for side in range(2):
+            rows = pl.ds(side * 128, 128)
+            first_out[1, d - 1, rows] = y_term(lax.rem(y + d, 4), side).reshape(128, QUARTER).astype(bf16)
+        first_copy(1, d).start()
+    xsum[...] = x_term(x)
+    for side in range(2):
+        ysum[side] = y_term(y, side)
 
     term_copy.wait()
     step_copy = remote(tbuf.at[0], tbuf.at[2], ts.at[1], tr.at[1], above)
     step_copy.start()
 
-    for copy in x_copies:
-        copy.wait_recv()
-    fsum[...] += (rx[0].astype(f32) + rx[1].astype(f32) + rx[2].astype(f32)).reshape(32, 8, HALF)
-
-    def y_part(to):
-        return fsum.reshape(8, 4, 8, HALF).at[:, to]
-
-    y_copies = []
+    for d in (1, 3, 2):
+        first_copy(0, d).wait_recv()
+        xsum[...] += first_in[0, d - 1].astype(f32).reshape(8, 4, 8, QUARTER)
+        first_copy(1, d).wait_recv()
+        ysum[...] += first_in[1, d - 1].astype(f32).reshape(2, 16, 8, QUARTER)
+
+    def second_copy(way, d):
+        i = way * 3 + d - 1
+        to = x_place(d) if way else y_place(d)
+        return remote(second_out.at[way, d - 1], second_in.at[way, d - 1], us.at[i], ur.at[i], to)
+
+    def x_rest(to):
+        return ysum[to // 2, pl.ds(lax.rem(to, 2) * 8, 8)]
+
     for d in (2, 1, 3):
-        copy = remote(y_part(lax.rem(y + d, 4)), ry.at[d - 1], us.at[d - 1], ur.at[d - 1], y_place(d))
-        copy.start()
-        y_copies.append(copy)
-    for copy in y_copies:
-        copy.wait_recv()
-    gsum[...] = y_part(y)[...] + ry[0] + ry[1] + ry[2]
+        second_out[0, d - 1] = xsum[:, lax.rem(y + d, 4)].reshape(64, QUARTER).astype(bf16)
+        second_copy(0, d).start()
+        second_out[1, d - 1] = x_rest(lax.rem(x + d, 4)).reshape(64, QUARTER).astype(bf16)
+        second_copy(1, d).start()
+    left, right = xsum[:, y], x_rest(x)
+    for d in (1, 3, 2):
+        second_copy(0, d).wait_recv()
+        left = left + second_in[0, d - 1].astype(f32).reshape(8, 8, QUARTER)
+        second_copy(1, d).wait_recv()
+        right = right + second_in[1, d - 1].astype(f32).reshape(8, 8, QUARTER)
+    gsum[:, :, :QUARTER] = left
+    gsum[:, :, QUARTER:] = right
 
     z_copies = []
     for d in (4, 3, 5, 2, 6, 1, 7):
@@ -213,9 +338,20 @@
     dens_ref[...] = total
 
     step_copy.wait_send()
-    core_copy.wait_send()
-    for copy in x_copies + y_copies + z_copies:
+    for copy in z_copies:
         copy.wait_send()
+    for way in range(2):
+        for d in range(1, 4):
+            first_copy(way, d).wait_send()
+            second_copy(way, d).wait_send()
+
+    @pl.loop(0, 4)
+    def _(i):
+        core_copy(i).wait_send()
+
+        @pl.when((i < 2) & (hands_on | hands_in))
+        def _():
+            handed_on(lax.rem(i, 2)).wait_send()
 
     @pl.loop(0, NC)
     def _(j):
@@ -240,25 +376,28 @@
             vmem((NAUX_HALF, NVIR), bf16),
             vmem((NVIR, NAUX_HALF), bf16),
             vmem((2, NC, NAUX_HALF, CW), bf16),
+            vmem((2, NAUX_HALF, CW), bf16),
             vmem((NC, NVIR, CW), bf16),
             vmem((NC, NVIR, CW), bf16),
             vmem((NC, NVIR, CW), f32),
             vmem((2, NVIR, NVIR), bf16),
             vmem((NVIR, NVIR), bf16),
-            vmem((64, 2, 8, NVIR), f32),
-            vmem((64, 8, NVIR), f32),
-            vmem((3, 256, HALF), bf16),
-            vmem((3, 256, HALF), bf16),
-            vmem((32, 8, HALF), f32),
-            vmem((3, 8, 8, HALF), f32),
+            vmem((16, 4, 2, 8, NVIR), f32),
+            vmem((16, 4, 8, NVIR), f32),
+            vmem((2, 3, 256, QUARTER), bf16),
+            vmem((2, 3, 256, QUARTER), bf16),
+            vmem((2, 3, 64, QUARTER), bf16),
+            vmem((2, 3, 64, QUARTER), bf16),
+            vmem((8, 4, 8, QUARTER), f32),
+            vmem((2, 16, 8, QUARTER), f32),
             vmem((8, 8, HALF), f32),
             vmem((7, 8, HALF), f32),
             vmem((3, 8, 128), f32),
             vmem((NVIR, 128), f32),
             dma(()),
             dma((NC,)), dma((NC,)), dma((NC,)), dma((NC,)), dma((NC,)), dma((NC,)),
-            dma(()), dma(()),
-            dma((3,)), dma((3,)), dma((3,)), dma((3,)), dma((7,)), dma((7,)), dma((2,)), dma((2,)),
+            dma((2,)), dma((2,)), dma((4,)), dma((4,)),
+            dma((6,)), dma((6,)), dma((6,)), dma((6,)), dma((7,)), dma((7,)), dma((2,)), dma((2,)),
         ],
         compiler_params=pltpu.CompilerParams(
             collective_id=0, has_side_effects=True, vmem_limit_bytes=58 * 2**20

time: 154 us -> 118 us (0.77)
  the two profiles are of different devices: /device:TPU:10 before, /device:TPU:2 now
where the time goes in v2:
time: 118 us; the launch traced here: 117 us
  Pallas kernels  114 us (97%)
  local copies, waits for them, and re-layouts  2.51 us (2%)
    pallas_call x1, Pallas kernels, per_device(): pl.pallas_call(kernel, out_shape=(jax.ShapeDtypeStruct((8, HALF), f32), j...  114 us

profile of v2, /device:TPU:2, one launch (start us, length us, event | category | flops | bytes accessed | tf_op | source)
XLA Modules:
  0.0 116.8 jit_solution(4473337271893038242)
XLA Ops:
  0.6 113.6 %shard_map.50 = (f32[8,512]{1,0:T(8,128)}, f32[8,128]{1,0:T(8,128)}) custom-call(bf16[1,2560,1024]{2,1,0:T(8,128)(2,1)} %x_ref.1, f32[128]{0:T(128)} %eocc_ref.1, f32[1,1024]{1,0:T(1,128)} %bitcast.2), custom_call_target="tpu_custom_call" | custom-call | flops 12999999488 | bytes 16000000 | tf_op jit(solution)/shard_map/pallas_call | solution.py:366
  114.3 1.2 %slice.3 = f32[1,1]{1,0:T(1,128)} slice(f32[8,128]{1,0:T(8,128)} %get-tuple-element.5), slice={[0:1], [0:1]} | slice | bytes 8 | tf_op jit(solution)/shard_map/slice | solution.py:407
  115.5 1.3 %copy.6 = f32[8,512]{1,0:T(8,128)} copy(f32[8,512]{1,0:T(8,128)} %get-tuple-element.8) | data formatting | bytes 32768

commit v3 on v2

--- a/solution.py
+++ b/solution.py
@@ -13,6 +13,7 @@
 NOCC = 128
 NC = 8
 CW = NVIR // NC
+LAG = 2
 HALF = NVIR // 2
 QUARTER = NVIR // 4
 f32 = jnp.float32
@@ -65,6 +66,7 @@
     hands_on = early_a | early_b
     hands_in = meets | late_a | late_b
     relay_from = jnp.where(early_a, 1, jnp.where(late_a, 3, jnp.where(late_b, 2, 0)))
+    relay_each = jnp.where(meets, 1, 2)
 
     def remote(src, dst, send, recv, device):
         return pltpu.make_async_remote_copy(
@@ -110,14 +112,14 @@
         place = corner_place(
             jnp.where(j < 4, low, 1 - low), jnp.where(j < 4, 0, 3), jnp.where(j < 4, 0, 5 - lax.rem(j, 2))
         )
-        slot = lax.rem(j // 2, 2)
+        slot = jnp.where(j < 4, lax.rem(j, 2), lax.rem(j // 2, 2))
         return remote(x_ref.at[0, :, columns(j)], relay.at[slot], ys.at[j], lw.at[slot], place)
 
     def handed_on(i):
         return remote(relay.at[i], relay.at[i], ls.at[i], lw.at[i], corner_place(low, 3, level - 3))
 
     def handed_in(i):
-        j = 2 * i + jnp.where(meets, 1, jnp.where(late_a, 5, 4))
+        j = jnp.where(meets, i, 2 * i + jnp.where(late_a, 5, 4))
         place = corner_place(jnp.where(meets, 1 - low, low), 0, 0)
         return remote(relay.at[i], blocks.at[0, j], ls.at[i], yr.at[j], place)
 
@@ -132,17 +134,15 @@
 
     @pl.loop(0, NC)
     def _(j):
-        i = j // 2
-        chunk = jnp.where(leaves, jnp.where(lax.rem(j, 2) == 0, i + 1 - 2 * lax.rem(i, 2), 4 + i), j)
-        by_relay = leaves & ((chunk >= 4) | (lax.rem(chunk, 2) == 1))
+        by_relay = leaves & ((j >= 4) | (j < 2))
 
         @pl.when(by_relay)
         def _():
-            relay_copy(chunk).start()
+            relay_copy(j).start()
 
         @pl.when(jnp.logical_not(by_relay))
         def _():
-            ring_copy(chunk).start()
+            ring_copy(j).start()
 
         @pl.when(core == 0)
         def _():
@@ -169,9 +169,8 @@
         pair_copy(j).wait_recv()
         vrow = v_ref[0:1, columns(j)]
 
-        @pl.loop(0, 8)
-        def _(m):
-            rows = pl.ds(pl.multiple_of(m * 128, 128), 128)
+        for m in range(8):
+            rows = pl.ds(m * 128, 128)
             total = acc[j, rows, :] + recvb[j, rows, :].astype(f32)
             part = total / (colv[rows, :] + vrow - center_energy - other_energy)
             lr[place, rows, columns(j)] = part.astype(bf16)
@@ -185,21 +184,6 @@
             @pl.when(up)
             def _():
                 pass_copy(j).start()
-
-            turn = j - relay_from
-            slot = lax.rem(jnp.maximum(turn, 0) // 2, 2)
-
-            @pl.when((hands_on | hands_in) & (turn >= 0) & (turn < 4) & (lax.rem(turn + 8, 2) == 0))
-            def _():
-                handed_on(slot).wait_recv()
-
-                @pl.when(hands_on)
-                def _():
-                    handed_on(slot).start()
-
-                @pl.when(hands_in)
-                def _():
-                    handed_in(slot).start()
 
         @pl.when(stream == 1)
         def _():
@@ -220,21 +204,43 @@
                 ).astype(bf16)
             pair_copy(j).start()
 
-    @pl.loop(0, NC + 1)
+    late_ring = meets
+    late_passed = (core == 0) & (y == 0) & (z == 0)
+    lag = jnp.where(late_ring | late_passed, LAG, 0)
+    sooner = jnp.where(late_ring, 1, jnp.where(late_passed, 0, 1 - h))
+
+    @pl.loop(0, NC + LAG + 1)
     def _(j):
         @pl.loop(0, 3)
         def _(q):
             early = up & (q < 2)
-            stream = jnp.where(up, jnp.where(early, 1, 0), jnp.where(q == 0, 1 - h, h))
-            chunk = jnp.where(early, 2 * j + q, j)
-
-            @pl.when((j < NC) & jnp.where(up, (q == 2) | (j < NC // 2), q < 2))
+            stream = jnp.where(up, jnp.where(early, 1, 0), jnp.where(q == 0, sooner, 1 - sooner))
+            turn = jnp.where(early, 2 * j + q, jnp.where(q == 0, j, j - lag))
+
+            @pl.when((turn >= 0) & (turn < NC) & (up | (q < 2)))
             def _():
-                product(stream, chunk)
-
-        @pl.when(j > 0)
-        def _():
-            finish(j - 1)
+                product(stream, turn)
+
+        since = j - relay_from
+        slot = jnp.where(since == 0, 0, 1)
+
+        @pl.when((hands_on | hands_in) & ((since == 0) | (since == relay_each)))
+        def _():
+            handed_on(slot).wait_recv()
+
+            @pl.when(hands_on)
+            def _():
+                handed_on(slot).start()
+
+            @pl.when(hands_in)
+            def _():
+                handed_in(slot).start()
+
+        done = j - 1 - lag
+
+        @pl.when((done >= 0) & (done < NC))
+        def _():
+            finish(done)
 
     def tilde_rows(i, term):
         rows = pl.ds(pl.multiple_of(i * 128, 128), 128)

time: 118 us -> 111 us (0.941)
  Pallas kernels: 114 us -> 107 us
    pallas_call x1, Pallas kernels: 114 us -> 107 us  [per_device(): pl.pallas_call(kernel, out_shape=(jax.ShapeDtypeStruct((8, HALF), f32), j...]
where the time goes in v3:
time: 111 us; the launch traced here: 110 us
  Pallas kernels  107 us (96%)
  local copies, waits for them, and re-layouts  2.51 us (2%)
    pallas_call x1, Pallas kernels, per_device(): pl.pallas_call(kernel, out_shape=(jax.ShapeDtypeStruct((8, HALF), f32), j...  107 us

profile of v3, /device:TPU:2, one launch (start us, length us, event | category | flops | bytes accessed | tf_op | source)
XLA Modules:
  0.0 109.9 jit_solution(14415472708702774131)
XLA Ops:
  0.6 106.8 %shard_map.50 = (f32[8,512]{1,0:T(8,128)}, f32[8,128]{1,0:T(8,128)}) custom-call(bf16[1,2560,1024]{2,1,0:T(8,128)(2,1)} %x_ref.1, f32[128]{0:T(128)} %eocc_ref.1, f32[1,1024]{1,0:T(1,128)} %bitcast.2), custom_call_target="tpu_custom_call" | custom-call | flops 12999999488 | bytes 16000000 | tf_op jit(solution)/shard_map/pallas_call | solution.py:372
  107.4 1.2 %slice.3 = f32[1,1]{1,0:T(1,128)} slice(f32[8,128]{1,0:T(8,128)} %get-tuple-element.5), slice={[0:1], [0:1]} | slice | bytes 8 | tf_op jit(solution)/shard_map/slice | solution.py:413
  108.6 1.3 %copy.6 = f32[8,512]{1,0:T(8,128)} copy(f32[8,512]{1,0:T(8,128)} %get-tuple-element.8) | data formatting | bytes 32768

commit v4 on v3

--- a/solution.py
+++ b/solution.py
@@ -14,6 +14,7 @@
 NC = 8
 CW = NVIR // NC
 LAG = 2
+PART = NAUX_HALF // 2
 HALF = NVIR // 2
 QUARTER = NVIR // 4
 f32 = jnp.float32
@@ -23,8 +24,8 @@
 def kernel(
     x_ref, eocc_ref, v_ref, dens_ref, diag_ref,
     own, own_t, blocks, relay, sendb, recvb, acc, lr, tt, dens, dens_in,
-    first_out, first_in, second_out, second_in, xsum, ysum, gsum, rz, tbuf, colv,
-    own_sem, ys, yr, ds, dr, xs, xr, ls, lw, cs, cr, fs, fr, us, ur, zs, zr, ts, tr,
+    x_out, x_in, y_out, y_in, second_out, second_in, xsum, ysum, gsum, rz, tbuf, colv,
+    own_sem, ys, yr, ds, dr, xs, xr, vs, ls, lw, cs, cr, fs, fr, gs, gr, us, ur, zs, zr, ts, tr,
 ):
     k = lax.axis_index("occ")
     h = lax.axis_index("aux")
@@ -65,7 +66,7 @@
     early_a, early_b, late_a, late_b = at(3, 4), at(3, 5), at(3, 1), at(3, 2)
     hands_on = early_a | early_b
     hands_in = meets | late_a | late_b
-    relay_from = jnp.where(early_a, 1, jnp.where(late_a, 3, jnp.where(late_b, 2, 0)))
+    relay_from = jnp.where(early_a, 1, jnp.where(late_a, 2, jnp.where(late_b, 1, 0)))
     relay_each = jnp.where(meets, 1, 2)
 
     def remote(src, dst, send, recv, device):
@@ -108,20 +109,28 @@
     def ring_copy(j):
         return remote(x_ref.at[0, :, columns(j)], blocks.at[0, j], ys.at[j], yr.at[j], onward)
 
-    def relay_copy(j):
+    def relay_copy(j, part):
         place = corner_place(
             jnp.where(j < 4, low, 1 - low), jnp.where(j < 4, 0, 3), jnp.where(j < 4, 0, 5 - lax.rem(j, 2))
         )
         slot = jnp.where(j < 4, lax.rem(j, 2), lax.rem(j // 2, 2))
-        return remote(x_ref.at[0, :, columns(j)], relay.at[slot], ys.at[j], lw.at[slot], place)
-
-    def handed_on(i):
-        return remote(relay.at[i], relay.at[i], ls.at[i], lw.at[i], corner_place(low, 3, level - 3))
-
-    def handed_in(i):
+        rows = pl.ds(part * PART, PART)
+        return remote(
+            x_ref.at[0, rows, columns(j)], relay.at[slot, rows], vs.at[2 * j + part], lw.at[2 * slot + part], place
+        )
+
+    def handed_on(i, part):
+        here = relay.at[i, pl.ds(part * PART, PART)]
+        return remote(here, here, ls.at[2 * i + part], lw.at[2 * i + part], corner_place(low, 3, level - 3))
+
+    def handed_in(i, part):
         j = jnp.where(meets, i, 2 * i + jnp.where(late_a, 5, 4))
         place = corner_place(jnp.where(meets, 1 - low, low), 0, 0)
-        return remote(relay.at[i], blocks.at[0, j], ls.at[i], yr.at[j], place)
+        rows = pl.ds(part * PART, PART)
+        return remote(relay.at[i, rows], blocks.at[0, j, rows], ls.at[2 * i + part], yr.at[j], place)
+
+    def by_relay(j):
+        return leaves & ((j >= 4) | (j < 2))
 
     def own_copy(j):
         return remote(x_ref.at[0, :, columns(j)], blocks.at[1, j], ds.at[j], dr.at[j], sibling)
@@ -134,13 +143,12 @@
 
     @pl.loop(0, NC)
     def _(j):
-        by_relay = leaves & ((j >= 4) | (j < 2))
-
-        @pl.when(by_relay)
-        def _():
-            relay_copy(j).start()
-
-        @pl.when(jnp.logical_not(by_relay))
+        @pl.when(by_relay(j))
+        def _():
+            for part in range(2):
+                relay_copy(j, part).start()
+
+        @pl.when(jnp.logical_not(by_relay(j)))
         def _():
             ring_copy(j).start()
 
@@ -175,6 +183,10 @@
             part = total / (colv[rows, :] + vrow - center_energy - other_energy)
             lr[place, rows, columns(j)] = part.astype(bf16)
             lr[1 - place, columns(j), rows] = part.T.astype(bf16)
+
+        strip = columns(j)
+        tt[strip, :] = (2.0 * lr[1, strip, :].astype(f32) - lr[0, strip, :].astype(f32)).astype(bf16)
+        tt[:, strip] = (2.0 * lr[1, :, strip].astype(f32) - lr[0, :, strip].astype(f32)).astype(bf16)
 
     def product(stream, j):
         @pl.when(stream == 0)
@@ -226,99 +238,112 @@
 
         @pl.when((hands_on | hands_in) & ((since == 0) | (since == relay_each)))
         def _():
-            handed_on(slot).wait_recv()
-
-            @pl.when(hands_on)
+            for part in range(2):
+                handed_on(slot, part).wait_recv()
+
+                @pl.when(hands_on)
+                def _():
+                    handed_on(slot, part).start()
+
+                @pl.when(hands_in)
+                def _():
+                    handed_in(slot, part).start()
+
+        done = j - 1 - lag
+
+        @pl.when((done >= 0) & (done < NC))
+        def _():
+            finish(done)
+
+    def term_rows(i, term):
+        rows = pl.ds(pl.multiple_of(i * 128, 128), 128)
+        product = lr[1, rows, :].astype(f32) * tt[rows, :].astype(f32)
+        return term + jnp.sum(product.reshape(16, 8, 8, 128), axis=(0, 2))
+
+    def quadrant(q):
+        d = jnp.where(q == 0, 2, jnp.where(q == 1, 1, jnp.where(q == 2, 3, 0)))
+        to = lax.rem(x + d, 4)
+        return d, to, lax.rem(to, 2), to // 2
+
+    def core_copy(q):
+        _, _, upper, side = quadrant(q)
+        rows = pl.ds(upper * 8, 8)
+        cols = pl.ds(pl.multiple_of(side * HALF, HALF), HALF)
+        return remote(
+            dens.at[rows, :, 1 - core, :, cols], dens_in.at[rows, :, :, cols], cs.at[q], cr.at[q], sibling
+        )
+
+    def x_copy(d):
+        return remote(x_out.at[d - 1], x_in.at[d - 1], fs.at[d - 1], fr.at[d - 1], x_place(d))
+
+    def y_copy(to, e):
+        return remote(y_out.at[e - 1, to], y_in.at[e - 1, to], gs.at[e - 1, to], gr.at[e - 1], y_place(e))
+
+    @pl.loop(0, 5)
+    def _(q):
+        @pl.when(q < 4)
+        def _():
+            _, _, upper, side = quadrant(q)
+            rows = pl.ds(pl.multiple_of(upper * HALF, HALF), HALF)
+            cols = pl.ds(pl.multiple_of(side * HALF, HALF), HALF)
+            out = 2.0 * jnp.dot(lr[0, rows, :], tt[:, cols], preferred_element_type=f32)
+            dens[pl.ds(upper * 8, 8), :, :, :, cols] = out.reshape(8, 4, 2, 8, HALF)
+            core_copy(q).start()
+
+        @pl.when(q > 0)
+        def _():
+            core_copy(q - 1).wait_recv()
+            d, to, upper, side = quadrant(q - 1)
+            rows = pl.ds(upper * 8, 8)
+            left = pl.ds(pl.multiple_of(side * HALF, QUARTER), QUARTER)
+            right = pl.ds(pl.multiple_of(side * HALF + QUARTER, QUARTER), QUARTER)
+            part = dens[rows, :, core, :, left] + dens_in[rows, :, :, left]
+
+            @pl.when(d == 0)
             def _():
-                handed_on(slot).start()
-
-            @pl.when(hands_in)
+                xsum[...] = part
+
+            @pl.when(d > 0)
             def _():
-                handed_in(slot).start()
-
-        done = j - 1 - lag
-
-        @pl.when((done >= 0) & (done < NC))
-        def _():
-            finish(done)
-
-    def tilde_rows(i, term):
-        rows = pl.ds(pl.multiple_of(i * 128, 128), 128)
-        left = lr[0, rows, :].astype(f32)
-        right = lr[1, rows, :].astype(f32)
-        tilde = (2.0 * right - left).astype(bf16)
-        tt[rows, :] = tilde
-        return term + jnp.sum((right * tilde.astype(f32)).reshape(16, 8, 8, 128), axis=(0, 2))
-
-    term = lax.fori_loop(0, 8, tilde_rows, jnp.zeros((8, 128), f32))
+                away = jnp.maximum(d, 1)
+                x_out[away - 1] = part.reshape(256, QUARTER).astype(bf16)
+                x_copy(away).start()
+
+            for e in (2, 1, 3, 0):
+                row = lax.rem(y + e, 4)
+                part = dens[rows, row, core, :, right] + dens_in[rows, row, :, right]
+                if e == 0:
+                    ysum[to] = part
+                else:
+                    y_out[e - 1, to] = part.reshape(64, QUARTER).astype(bf16)
+                    y_copy(to, e).start()
+
+    term = lax.fori_loop(0, 8, term_rows, jnp.zeros((8, 128), f32))
     tbuf[h] = jnp.full((8, 128), -(2.0 / NVIR) * jnp.sum(term), f32)
     term_copy = remote(tbuf.at[h], tbuf.at[h], ts.at[0], tr.at[0], partner)
     term_copy.start()
 
-    def core_copy(i):
-        rows = pl.ds(i * 4, 4)
-        return remote(dens.at[rows, :, 1 - core], dens_in.at[rows], cs.at[i], cr.at[i], sibling)
-
-    @pl.loop(0, 4)
-    def _(i):
-        rows = pl.ds(pl.multiple_of(i * 256, 256), 256)
-        out = 2.0 * jnp.dot(lr[0, rows, :], tt[...], preferred_element_type=f32)
-        dens[pl.ds(i * 4, 4)] = out.reshape(4, 4, 2, 8, NVIR)
-        core_copy(i).start()
-
-    @pl.loop(0, 4)
-    def _(i):
-        core_copy(i).wait_recv()
-
-    def x_term(to):
-        rows = pl.ds(lax.rem(to, 2) * 8, 8)
-        cols = pl.ds(pl.multiple_of((to // 2) * HALF, QUARTER), QUARTER)
-        return dens[rows, :, core, :, cols] + dens_in[rows, :, :, cols]
-
-    def y_term(to, side):
-        cols = pl.ds(side * HALF + QUARTER, QUARTER)
-        return dens[:, to, core, :, cols] + dens_in[:, to, :, cols]
-
-    def first_copy(way, d):
-        i = way * 3 + d - 1
-        to = y_place(d) if way else x_place(d)
-        return remote(first_out.at[way, d - 1], first_in.at[way, d - 1], fs.at[i], fr.at[i], to)
-
-    for d in (2, 1, 3):
-        first_out[0, d - 1] = x_term(lax.rem(x + d, 4)).reshape(256, QUARTER).astype(bf16)
-        first_copy(0, d).start()
-        for side in range(2):
-            rows = pl.ds(side * 128, 128)
-            first_out[1, d - 1, rows] = y_term(lax.rem(y + d, 4), side).reshape(128, QUARTER).astype(bf16)
-        first_copy(1, d).start()
-    xsum[...] = x_term(x)
-    for side in range(2):
-        ysum[side] = y_term(y, side)
-
-    term_copy.wait()
-    step_copy = remote(tbuf.at[0], tbuf.at[2], ts.at[1], tr.at[1], above)
-    step_copy.start()
-
     for d in (1, 3, 2):
-        first_copy(0, d).wait_recv()
-        xsum[...] += first_in[0, d - 1].astype(f32).reshape(8, 4, 8, QUARTER)
-        first_copy(1, d).wait_recv()
-        ysum[...] += first_in[1, d - 1].astype(f32).reshape(2, 16, 8, QUARTER)
+        x_copy(d).wait_recv()
+        xsum[...] += x_in[d - 1].astype(f32).reshape(8, 4, 8, QUARTER)
+        remote(y_out.at[d - 1], y_in.at[d - 1], gs.at[d - 1, 0], gr.at[d - 1], y_place(d)).wait_recv()
+        ysum[...] += y_in[d - 1].astype(f32).reshape(4, 8, 8, QUARTER)
 
     def second_copy(way, d):
         i = way * 3 + d - 1
         to = x_place(d) if way else y_place(d)
         return remote(second_out.at[way, d - 1], second_in.at[way, d - 1], us.at[i], ur.at[i], to)
 
-    def x_rest(to):
-        return ysum[to // 2, pl.ds(lax.rem(to, 2) * 8, 8)]
-
     for d in (2, 1, 3):
         second_out[0, d - 1] = xsum[:, lax.rem(y + d, 4)].reshape(64, QUARTER).astype(bf16)
         second_copy(0, d).start()
-        second_out[1, d - 1] = x_rest(lax.rem(x + d, 4)).reshape(64, QUARTER).astype(bf16)
+        second_out[1, d - 1] = ysum[lax.rem(x + d, 4)].reshape(64, QUARTER).astype(bf16)
         second_copy(1, d).start()
-    left, right = xsum[:, y], x_rest(x)
+    term_copy.wait()
+    step_copy = remote(tbuf.at[0], tbuf.at[2], ts.at[1], tr.at[1], above)
+    step_copy.start()
+
+    left, right = xsum[:, y], ysum[x]
     for d in (1, 3, 2):
         second_copy(0, d).wait_recv()
         left = left + second_in[0, d - 1].astype(f32).reshape(8, 8, QUARTER)
@@ -348,20 +373,32 @@
         copy.wait_send()
     for way in range(2):
         for d in range(1, 4):
-            first_copy(way, d).wait_send()
             second_copy(way, d).wait_send()
+    for d in range(1, 4):
+        x_copy(d).wait_send()
 
     @pl.loop(0, 4)
     def _(i):
         core_copy(i).wait_send()
+        for e in range(1, 4):
+            y_copy(i, e).wait_send()
 
         @pl.when((i < 2) & (hands_on | hands_in))
         def _():
-            handed_on(lax.rem(i, 2)).wait_send()
+            for part in range(2):
+                handed_on(lax.rem(i, 2), part).wait_send()
 
     @pl.loop(0, NC)
     def _(j):
-        ring_copy(j).wait_send()
+        @pl.when(by_relay(j))
+        def _():
+            for part in range(2):
+                relay_copy(j, part).wait_send()
+
+        @pl.when(jnp.logical_not(by_relay(j)))
+        def _():
+            ring_copy(j).wait_send()
+
         own_copy(j).wait_send()
         pair_copy(j).wait_send()
 
@@ -390,20 +427,22 @@
             vmem((NVIR, NVIR), bf16),
             vmem((16, 4, 2, 8, NVIR), f32),
             vmem((16, 4, 8, NVIR), f32),
-            vmem((2, 3, 256, QUARTER), bf16),
-            vmem((2, 3, 256, QUARTER), bf16),
+            vmem((3, 256, QUARTER), bf16),
+            vmem((3, 256, QUARTER), bf16),
+            vmem((3, 4, 64, QUARTER), bf16),
+            vmem((3, 4, 64, QUARTER), bf16),
             vmem((2, 3, 64, QUARTER), bf16),
             vmem((2, 3, 64, QUARTER), bf16),
             vmem((8, 4, 8, QUARTER), f32),
-            vmem((2, 16, 8, QUARTER), f32),
+            vmem((4, 8, 8, QUARTER), f32),
             vmem((8, 8, HALF), f32),
             vmem((7, 8, HALF), f32),
             vmem((3, 8, 128), f32),
             vmem((NVIR, 128), f32),
             dma(()),
             dma((NC,)), dma((NC,)), dma((NC,)), dma((NC,)), dma((NC,)), dma((NC,)),
-            dma((2,)), dma((2,)), dma((4,)), dma((4,)),
-            dma((6,)), dma((6,)), dma((6,)), dma((6,)), dma((7,)), dma((7,)), dma((2,)), dma((2,)),
+            dma((2 * NC,)), dma((4,)), dma((4,)), dma((4,)), dma((4,)),
+            dma((3,)), dma((3,)), dma((3, 4)), dma((3,)), dma((6,)), dma((6,)), dma((7,)), dma((7,)), dma((2,)), dma((2,)),
         ],
         compiler_params=pltpu.CompilerParams(
             collective_id=0, has_side_effects=True, vmem_limit_bytes=58 * 2**20

time: 111 us -> 109 us (0.982)
  Pallas kernels: 107 us -> 105 us
    pallas_call x1, Pallas kernels: 107 us -> 105 us  [per_device(): pl.pallas_call(kernel, out_shape=(jax.ShapeDtypeStruct((8, HALF), f32), j...]
where the time goes in v4:
time: 109 us; the launch traced here: 108 us
  Pallas kernels  105 us (96%)
  local copies, waits for them, and re-layouts  2.51 us (2%)
    pallas_call x1, Pallas kernels, per_device(): pl.pallas_call(kernel, out_shape=(jax.ShapeDtypeStruct((8, HALF), f32), j...  105 us

profile of v4, /device:TPU:2, one launch (start us, length us, event | category | flops | bytes accessed | tf_op | source)
XLA Modules:
  0.0 108.4 jit_solution(3938264976069827398)
XLA Ops:
  0.6 105.3 %shard_map.50 = (f32[8,512]{1,0:T(8,128)}, f32[8,128]{1,0:T(8,128)}) custom-call(bf16[1,2560,1024]{2,1,0:T(8,128)(2,1)} %x_ref.1, f32[128]{0:T(128)} %eocc_ref.1, f32[1,1024]{1,0:T(1,128)} %bitcast.2), custom_call_target="tpu_custom_call" | custom-call | flops 12999999488 | bytes 16000000 | tf_op jit(solution)/shard_map/pallas_call | solution.py:409
  105.9 1.2 %slice.3 = f32[1,1]{1,0:T(1,128)} slice(f32[8,128]{1,0:T(8,128)} %get-tuple-element.5), slice={[0:1], [0:1]} | slice | bytes 8 | tf_op jit(solution)/shard_map/slice | solution.py:452
  107.1 1.3 %copy.6 = f32[8,512]{1,0:T(8,128)} copy(f32[8,512]{1,0:T(8,128)} %get-tuple-element.8) | data formatting | bytes 32768

commit v5 on v4

--- a/solution.py
+++ b/solution.py
@@ -78,8 +78,8 @@
     load.start()
 
     barrier = pltpu.get_barrier_semaphore()
-    greeted = [above, below, sibling, partner, x_place(1), x_place(3)]
-    greeted += [y_place(d) for d in range(1, 4)] + [z_place(d) for d in range(1, 8)]
+    greeted = [z_place(d) for d in (4, 3, 5, 2, 6, 1, 7)] + [y_place(d) for d in (2, 1, 3)]
+    greeted += [partner, x_place(1), x_place(3), above, below, sibling]
     for device in greeted:
         pl.semaphore_signal(barrier, inc=1, device_id=device, device_id_type=MESH)
 
@@ -358,6 +358,37 @@
         copy.start()
         z_copies.append(copy)
 
+    for way in range(2):
+        for d in range(1, 4):
+            second_copy(way, d).wait_send()
+    for d in range(1, 4):
+        x_copy(d).wait_send()
+
+    @pl.loop(0, 4)
+    def _(i):
+        core_copy(i).wait_send()
+        for e in range(1, 4):
+            y_copy(i, e).wait_send()
+
+        @pl.when((i < 2) & (hands_on | hands_in))
+        def _():
+            for part in range(2):
+                handed_on(lax.rem(i, 2), part).wait_send()
+
+    @pl.loop(0, NC)
+    def _(j):
+        @pl.when(by_relay(j))
+        def _():
+            for part in range(2):
+                relay_copy(j, part).wait_send()
+
+        @pl.when(jnp.logical_not(by_relay(j)))
+        def _():
+            ring_copy(j).wait_send()
+
+        own_copy(j).wait_send()
+        pair_copy(j).wait_send()
+
     step_copy.wait_recv()
     diag_ref[...] = tbuf[1] + jnp.where(core == 0, tbuf[2], tbuf[0])
 
@@ -371,36 +402,11 @@
     step_copy.wait_send()
     for copy in z_copies:
         copy.wait_send()
-    for way in range(2):
-        for d in range(1, 4):
-            second_copy(way, d).wait_send()
-    for d in range(1, 4):
-        x_copy(d).wait_send()
-
-    @pl.loop(0, 4)
-    def _(i):
-        core_copy(i).wait_send()
-        for e in range(1, 4):
-            y_copy(i, e).wait_send()
-
-        @pl.when((i < 2) & (hands_on | hands_in))
-        def _():
-            for part in range(2):
-                handed_on(lax.rem(i, 2), part).wait_send()
-
-    @pl.loop(0, NC)
-    def _(j):
-        @pl.when(by_relay(j))
-        def _():
-            for part in range(2):
-                relay_copy(j, part).wait_send()
-
-        @pl.when(jnp.logical_not(by_relay(j)))
-        def _():
-            ring_copy(j).wait_send()
-
-        own_copy(j).wait_send()
-        pair_copy(j).wait_send()
+
+
+def hand_over(dens_in_ref, diag_in_ref, dens_ref, diag_ref):
+    dens_ref[...] = dens_in_ref[...]
+    diag_ref[0] = diag_in_ref[0, 0]
 
 
 def per_device(cholesky, occ_energy, vir_energy):
@@ -449,7 +455,12 @@
         ),
         cost_estimate=pl.CostEstimate(flops=13_000_000_000, bytes_accessed=16_000_000, transcendentals=0),
     )(cholesky, occ_energy, vir_energy.reshape(1, NVIR))
-    return dens, diag[0, :1]
+    return pl.pallas_call(
+        hand_over,
+        out_shape=(jax.ShapeDtypeStruct((8, HALF), f32), jax.ShapeDtypeStruct((1,), f32)),
+        in_specs=[pl.BlockSpec(memory_space=pltpu.VMEM), pl.BlockSpec(memory_space=pltpu.VMEM)],
+        out_specs=(pl.BlockSpec(memory_space=pltpu.VMEM), pl.BlockSpec(memory_space=pltpu.SMEM)),
+    )(dens, diag)
 
 
 def solution(mesh):

time: 109 us -> 107 us (0.982)
  local copies, waits for them, and re-layouts: 2.51 us -> 0 us
  Pallas kernels: 105 us -> 107 us
    pallas_call x0 -> x1, Pallas kernels: none -> 1.34 us  [per_device(): pl.pallas_call(hand_over, out_shape=(jax.ShapeDtypeStruct((8, HALF), f32)...]
    unnamed x1 -> x0, local copies, waits for them, and re-layouts: 1.32 us -> none
    slice x1 -> x0, local copies, waits for them, and re-layouts: 1.18 us -> none  [per_device(): return (dens, diag[0, :1])]
where the time goes in v5:
time: 107 us
  Pallas kernels  107 us (100%)
    pallas_call x1, Pallas kernels, per_device(): pl.pallas_call(kernel, out_shape=(jax.ShapeDtypeStruct((8, HALF), f32), j...  105 us

profile of v5, /device:TPU:2, one launch (start us, length us, event | category | flops | bytes accessed | tf_op | source)
XLA Modules:
  0.0 107.2 jit_solution(15056536167080109748)
XLA Ops:
  0.6 105.2 %shard_map.50 = (f32[8,512]{1,0:T(8,128)}, f32[8,128]{1,0:T(8,128)}) custom-call(bf16[1,2560,1024]{2,1,0:T(8,128)(2,1)} %x_ref.1, f32[128]{0:T(128)} %eocc_ref.1, f32[1,1024]{1,0:T(1,128)} %bitcast.1), custom_call_target="tpu_custom_call" | custom-call | flops 12999999488 | bytes 16000000 | tf_op jit(solution)/shard_map/pallas_call | solution.py:415
  105.8 1.3 %shard_map.51 = (f32[8,512]{1,0:T(8,128)}, f32[1]{0:T(128)}) custom-call(f32[8,512]{1,0:T(8,128)} %get-tuple-element.4.dens_in_ref, f32[8,128]{1,0:T(8,128)} %get-tuple-element.5.diag_in_ref), custom_call_target="tpu_custom_call" | custom-call | tf_op jit(solution)/shard_map/pallas_call | solution.py:458

commit v6 on v5

--- a/solution.py
+++ b/solution.py
@@ -121,7 +121,8 @@
 
     def handed_on(i, part):
         here = relay.at[i, pl.ds(part * PART, PART)]
-        return remote(here, here, ls.at[2 * i + part], lw.at[2 * i + part], corner_place(low, 3, level - 3))
+        place = corner_place(low, 3, jnp.where(hands_on, level - 3, level))
+        return remote(here, here, ls.at[2 * i + part], lw.at[2 * i + part], place)
 
     def handed_in(i, part):
         j = jnp.where(meets, i, 2 * i + jnp.where(late_a, 5, 4))

time: 107 us -> 107 us (level)
  no operation moved by 1% of the time
where the time goes in v6:
time: 107 us
  Pallas kernels  106 us (99%)
    pallas_call x1, Pallas kernels, per_device(): pl.pallas_call(kernel, out_shape=(jax.ShapeDtypeStruct((8, HALF), f32), j...  105 us

profile of v6, /device:TPU:2, one launch (start us, length us, event | category | flops | bytes accessed | tf_op | source)
XLA Modules:
  0.0 107.1 jit_solution(835681788598327178)
XLA Ops:
  0.6 105.1 %shard_map.50 = (f32[8,512]{1,0:T(8,128)}, f32[8,128]{1,0:T(8,128)}) custom-call(bf16[1,2560,1024]{2,1,0:T(8,128)(2,1)} %x_ref.1, f32[128]{0:T(128)} %eocc_ref.1, f32[1,1024]{1,0:T(1,128)} %bitcast.1), custom_call_target="tpu_custom_call" | custom-call | flops 12999999488 | bytes 16000000 | tf_op jit(solution)/shard_map/pallas_call | solution.py:416
  105.7 1.3 %shard_map.51 = (f32[8,512]{1,0:T(8,128)}, f32[1]{0:T(128)}) custom-call(f32[8,512]{1,0:T(8,128)} %get-tuple-element.4.dens_in_ref, f32[8,128]{1,0:T(8,128)} %get-tuple-element.5.diag_in_ref), custom_call_target="tpu_custom_call" | custom-call | tf_op jit(solution)/shard_map/pallas_call | solution.py:459

commit v7 on v6

--- a/solution.py
+++ b/solution.py
@@ -287,7 +287,7 @@
             _, _, upper, side = quadrant(q)
             rows = pl.ds(pl.multiple_of(upper * HALF, HALF), HALF)
             cols = pl.ds(pl.multiple_of(side * HALF, HALF), HALF)
-            out = 2.0 * jnp.dot(lr[0, rows, :], tt[:, cols], preferred_element_type=f32)
+            out = jnp.dot(lr[0, rows, :], tt[:, cols], preferred_element_type=f32)
             dens[pl.ds(upper * 8, 8), :, :, :, cols] = out.reshape(8, 4, 2, 8, HALF)
             core_copy(q).start()
 
@@ -398,7 +398,7 @@
     total = gsum[z]
     for d in range(7):
         total = total + rz[d]
-    dens_ref[...] = total
+    dens_ref[...] = 2.0 * total
 
     step_copy.wait_send()
     for copy in z_copies:

time: 107 us -> 107 us (level)
  no operation moved by 1% of the time
where the time goes in v7:
time: 107 us
  Pallas kernels  106 us (99%)
    pallas_call x1, Pallas kernels, per_device(): pl.pallas_call(kernel, out_shape=(jax.ShapeDtypeStruct((8, HALF), f32), j...  105 us

profile of v7, /device:TPU:2, one launch (start us, length us, event | category | flops | bytes accessed | tf_op | source)
XLA Modules:
  0.0 107.1 jit_solution(808980150552328256)
XLA Ops:
  0.6 105.1 %shard_map.50 = (f32[8,512]{1,0:T(8,128)}, f32[8,128]{1,0:T(8,128)}) custom-call(bf16[1,2560,1024]{2,1,0:T(8,128)(2,1)} %x_ref.1, f32[128]{0:T(128)} %eocc_ref.1, f32[1,1024]{1,0:T(1,128)} %bitcast.1), custom_call_target="tpu_custom_call" | custom-call | flops 12999999488 | bytes 16000000 | tf_op jit(solution)/shard_map/pallas_call | solution.py:416
  105.7 1.3 %shard_map.51 = (f32[8,512]{1,0:T(8,128)}, f32[1]{0:T(128)}) custom-call(f32[8,512]{1,0:T(8,128)} %get-tuple-element.4.dens_in_ref, f32[8,128]{1,0:T(8,128)} %get-tuple-element.5.diag_in_ref), custom_call_target="tpu_custom_call" | custom-call | tf_op jit(solution)/shard_map/pallas_call | solution.py:459
